TPU v7x, 128 devices: a whole 4x4x4 slice. The times are simulated.
128 devices in a mesh: rep: 16 (over z_lo, x, core), grp: 8 (over z_hi, y).
Axes of the slice: x: 4, y: 4, z: 4 (z_hi: 2, z_lo: 2; z = z_hi * 2 + z_lo), core: 2. Of those that a mesh axis runs over, the one named last changes fastest.
Arguments:
- tokens: bfloat16 [32, 1024, 1024], P('rep', 'grp'), may hold values from -6 to 6
- segments: int32 [32, 1024], P('rep'), may hold values from 0 to 2, as said below
- routes: int32 [32, 1024, 2], P('rep', 'grp'), may hold values from 0 to 5, all different within a row
- cotangent: bfloat16 [32, 1024, 1024], P('rep', 'grp'), may hold values from -6 to 6
- w_qkv: float32 [1024, 2048], P('grp'), may hold values from -0.1875 to 0.1875
- w_out: float32 [1024, 1024], P('grp'), may hold values from -1.5 to 1.5
- w_gateup: float32 [6, 1024, 1024], P(None, 'grp'), may hold values from -0.1875 to 0.1875
- w_down: float32 [6, 512, 1024], P(None, None, 'grp'), may hold values from -0.5 to 0.5
- w_router: float32 [1024, 6], P('grp'), may hold values from -0.09375 to 0.09375
- w_gains: float32 [2, 1024], P(None, 'grp'), may hold values from 0.5 to 1.5
- qkv_first: float32 [1024, 2048], P('grp'), may hold values from -192 to 192
- qkv_second: float32 [1024, 2048], P('grp'), may hold values from 1966.08 to 15400.96
- out_first: float32 [1024, 1024], P('grp'), may hold values from -20 to 20
- out_second: float32 [1024, 1024], P('grp'), may hold values from 19.6608 to 154.0096
- gateup_first: float32 [6, 1024, 1024], P(None, 'grp'), may hold values from -48 to 48
- gateup_second: float32 [6, 1024, 1024], P(None, 'grp'), may hold values from 137.6256 to 1114.112
- down_first: float32 [6, 512, 1024], P(None, None, 'grp'), may hold values from -20 to 20
- down_second: float32 [6, 512, 1024], P(None, None, 'grp'), may hold values from 19.6608 to 154.0096
- router_first: float32 [1024, 6], P('grp'), may hold values from -1280 to 1280
- router_second: float32 [1024, 6], P('grp'), may hold values from 107374.18 to 872415.25
- gains_first: float32 [2, 1024], P(None, 'grp'), may hold values from -192 to 192
- gains_second: float32 [2, 1024], P(None, 'grp'), may hold values from 1966.08 to 15400.96
Outputs:
- layer_out: bfloat16 [32, 1024, 1024], P('rep', 'grp')
- input_grad: float32 [32, 1024, 1024], P('rep', 'grp')
- qkv_moment: float32 [1024, 2048], P('grp')
- qkv_square: float32 [1024, 2048], P('grp')
- qkv_updated: float32 [1024, 2048], P('grp')
- out_moment: float32 [1024, 1024], P('grp')
- out_square: float32 [1024, 1024], P('grp')
- out_updated: float32 [1024, 1024], P('grp')
- gateup_moment: float32 [6, 1024, 1024], P(None, 'grp')
- gateup_square: float32 [6, 1024, 1024], P(None, 'grp')
- gateup_updated: float32 [6, 1024, 1024], P(None, 'grp')
- down_moment: float32 [6, 512, 1024], P(None, None, 'grp')
- down_square: float32 [6, 512, 1024], P(None, None, 'grp')
- down_updated: float32 [6, 512, 1024], P(None, None, 'grp')
- router_moment: float32 [1024, 6], P('grp')
- router_square: float32 [1024, 6], P('grp')
- router_updated: float32 [1024, 6], P('grp')
- gains_moment: float32 [2, 1024], P(None, 'grp')
- gains_square: float32 [2, 1024], P(None, 'grp')
- gains_updated: float32 [2, 1024], P(None, 'grp')
Inputs may be any that keep to these rules, and one draw needn't show every extreme that they name: `routes`: each token names 2 different experts. `segments`: a sequence's segment numbers start at 0 and never fall; of each 2 consecutive sequences one is a single document.
All inputs are finite; a program needn't handle non-finite values.
Results may differ from a plain program's by a relative error of at most 0.034.
Values may be sent and summed in bfloat16 or wider, within the bound.
A program may use at most 256 MiB of HBM per device.

v0:
```python
import jax
import jax.numpy as jnp
import numpy as np
from jax import lax
from jax.experimental import pallas as pl
from jax.experimental.pallas import tpu as pltpu
from jax.sharding import PartitionSpec as P

D = 1024
HQ = 16
HK = 8
HD = 64
FF = 512
EXPERTS = 6
TOPK = 2
STEP = 10
ROWS = 256
SLICE = 64
WIDE = EXPERTS * SLICE

beta_one = 0.9
beta_two = 0.95
adam_epsilon = 1e-08
norm_epsilon = 1e-06

f32 = jnp.float32
b16 = jnp.bfloat16
MESH = pl.DeviceIdType.MESH
ANY = pl.BlockSpec(memory_space=pl.ANY)
VMEM = pl.BlockSpec(memory_space=pltpu.VMEM)
MIB = 2**20


def place():
    rep = lax.axis_index("rep")
    grp = lax.axis_index("grp")
    z_lo, x, c = rep // 8, lax.rem(rep // 2, 4), lax.rem(rep, 2)
    z_hi, y = grp // 4, lax.rem(grp, 4)
    return x, y, z_hi * 2 + z_lo, c


def dev(x, y, z, c):
    x, y, z = lax.rem(x + 4, 4), lax.rem(y + 4, 4), lax.rem(z + 4, 4)
    return (lax.rem(z, 2) * 8 + x * 2 + c, (z // 2) * 4 + y)


class Net:
    def __init__(self, send_sems, recv_sems, local_sems):
        self.sems = (send_sems, recv_sems, local_sems)
        self.count = 0
        self.locals = 0
        self.open = []

    def call(self, peers):
        self.peers = len(peers)
        for peer in peers:
            pl.semaphore_signal(pltpu.get_barrier_semaphore(), inc=1, device_id=peer, device_id_type=MESH)

    def answer(self):
        pl.semaphore_wait(pltpu.get_barrier_semaphore(), self.peers)

    def greet(self, peers):
        self.call(peers)
        self.answer()

    def describe(self, n, src, dst, peer):
        return pltpu.make_async_remote_copy(
            src_ref=src,
            dst_ref=dst,
            send_sem=self.sems[0].at[n],
            recv_sem=self.sems[1].at[n],
            device_id=peer,
            device_id_type=MESH,
        )

    def planned(self, src, dst, peer):
        copy = self.describe(self.count, src, dst, peer)
        self.count += 1
        self.open.append(copy)
        return copy

    def send(self, src, dst, peer):
        copy = self.planned(src, dst, peer)
        copy.start()
        return copy

    def local(self, src, dst):
        copy = pltpu.make_async_copy(src, dst, self.sems[2].at[self.locals])
        copy.start()
        self.locals += 1
        return copy

    def got(self, copy):
        copy.wait_recv()
        copy.seen = True

    def gone(self, copy):
        copy.wait_send()
        copy.left = True

    def finish(self):
        for copy in self.open:
            if not getattr(copy, "seen", False):
                copy.wait_recv()
            if not getattr(copy, "left", False):
                copy.wait_send()


def sems(n, n_local=1):
    return [
        pltpu.SemaphoreType.DMA((n,)),
        pltpu.SemaphoreType.DMA((n,)),
        pltpu.SemaphoreType.DMA((n_local,)),
    ]


def params(cid=None, mib=56):
    if cid is None:
        return pltpu.CompilerParams(vmem_limit_bytes=mib * MIB)
    return pltpu.CompilerParams(
        vmem_limit_bytes=mib * MIB, collective_id=cid, has_side_effects=True
    )


def shape(dims, dtype):
    return jax.ShapeDtypeStruct(dims, dtype)


class Ring:
    def __init__(self, net, part, right, left, me):
        self.net, self.part, self.right, self.left = net, part, right, left
        self.before, self.after = lax.rem(me + 3, 4), lax.rem(me + 1, 4)
        self.a1 = net.send(part(me, 0), part(me, 0), right)
        self.b1 = net.send(part(me, 1), part(me, 1), left)
        self.rest = [
            net.send(part(me, 1), part(me, 1), right),
            net.send(part(me, 0), part(me, 0), left),
        ]

    def relay(self):
        net, part = self.net, self.part
        net.got(self.a1)
        self.rest.append(net.send(part(self.before, 0), part(self.before, 0), self.right))
        net.got(self.b1)
        self.rest.append(net.send(part(self.after, 1), part(self.after, 1), self.left))

    def done(self):
        for copy in self.rest:
            self.net.got(copy)


def add_rows(dst, one, two, rows, step):
    def body(i, carry):
        at = pl.ds(pl.multiple_of(i * step, step), step)
        dst[at] = (one[at].astype(f32) + two[at].astype(f32)).astype(b16)
        return carry

    lax.fori_loop(0, rows // step, body, 0)


class Scatter:
    def __init__(self, net, part, tmp, got, right, left, me, rows, step, begin=True):
        self.net, self.part, self.tmp, self.got = net, part, tmp, got
        self.right, self.left, self.me, self.step = right, left, me, step
        self.half = rows // 2
        self.lo, self.hi = pl.ds(0, self.half), pl.ds(self.half, self.half)
        self.after, self.before = lax.rem(me + 1, 4), lax.rem(me + 3, 4)
        self.first, self.rest = [], []
        if begin:
            across = part(lax.rem(me + 2, 4))
            self.first = [net.send(across.at[self.lo], tmp.at[0], right), net.send(across.at[self.hi], tmp.at[1], left)]
            self.rest = [
                net.send(part(self.after).at[self.hi], got.at[0, self.hi], right),
                net.send(part(self.before).at[self.lo], got.at[1, self.lo], left),
            ]

    def relay(self):
        net, tmp, got = self.net, self.tmp, self.got
        for copy in self.first[:1]:
            net.got(copy)
        add_rows(tmp.at[0], tmp.at[0], self.part(self.after).at[self.lo], self.half, self.step)
        self.rest.append(net.send(tmp.at[0], got.at[0, self.lo], self.right))
        for copy in self.first[1:]:
            net.got(copy)
        add_rows(tmp.at[1], tmp.at[1], self.part(self.before).at[self.hi], self.half, self.step)
        self.rest.append(net.send(tmp.at[1], got.at[1, self.hi], self.left))

    def done(self):
        for copy in self.rest:
            self.net.got(copy)

    def term(self, at):
        own = self.part(self.me)
        return own[at].astype(f32) + self.got[0, at].astype(f32) + self.got[1, at].astype(f32)

    def settle(self, dst, rows, step):
        def body(i, carry):
            at = pl.ds(pl.multiple_of(i * step, step), step)
            dst[at] = self.term(at).astype(dst.dtype)
            return carry

        lax.fori_loop(0, rows // step, body, 0)


def dot(a, b):
    return lax.dot_general(a, b, (((1,), (0,)), ((), ())), preferred_element_type=f32)


def dot_t(a, b):
    return lax.dot_general(a, b, (((1,), (1,)), ((), ())), preferred_element_type=f32)


def t_dot(a, b):
    return lax.dot_general(a, b, (((0,), (0,)), ((), ())), preferred_element_type=f32)


def partner_lanes(v):
    lane = lax.broadcasted_iota(jnp.int32, v.shape, 1)
    return jnp.where(lane % HD < HD // 2, pltpu.roll(v, 96, 1), pltpu.roll(v, 32, 1))


def half_mask(rows, half):
    lane = lax.broadcasted_iota(jnp.int32, (rows, 128), 1)
    return (lane < HD) if half == 0 else (lane >= HD)


def spread(tile, half):
    keep = half_mask(ROWS, half)
    heads = []
    for g in range(2):
        v = tile if g == half else pltpu.roll(tile, HD, 1)
        heads.append(jnp.where(keep, v, 0.0).astype(b16))
    low = jnp.concatenate([h[:128] for h in heads], axis=0)
    high = jnp.concatenate([h[128:] for h in heads], axis=0)
    return low, high


def collect(low, high, half):
    heads = []
    for g in range(2):
        v = jnp.concatenate([low[g * 128 : g * 128 + 128], high[g * 128 : g * 128 + 128]], axis=0)
        heads.append(v if g == half else pltpu.roll(v, HD, 1))
    return jnp.where(half_mask(ROWS, 0), heads[0], heads[1])


def router_rows(tail):
    row = lax.broadcasted_iota(jnp.int32, (16, D), 0)
    kept = jnp.where(row < EXPERTS, tail.astype(f32), 0.0).astype(b16)
    return jnp.concatenate([kept, jnp.zeros((112, D), b16)], axis=0)


def one_hot(routes, slot):
    lane = lax.broadcasted_iota(jnp.int32, (ROWS, 128), 1)
    return (routes[:, slot : slot + 1] == lane).astype(f32)


def lanes(n, width=128):
    return pl.ds(pl.multiple_of(n * width, width), width)


class Fan:
    def __init__(self, net, src, at, shards, over, ys):
        self.net, self.src, self.at, self.ys, self.shards = net, src, at, ys, shards
        self.over = net.send(src, at(shards[0]), over)

    def round(self):
        self.out = [self.net.send(self.src, self.at(self.shards[0]), p) for p in self.ys]
        return self

    def forward(self):
        self.net.got(self.over)
        ref = self.at(self.shards[1])
        self.out += [self.net.send(ref, ref, p) for p in self.ys]
        return ref

    def arrivals(self):
        for copy, n in zip(self.out, self.shards[2:]):
            self.net.got(copy)
            yield self.at(n)


def front_kernel(
    tok, cot, rl, wqkv, wout, wgu, wdn, cos_t, sin_t, router, gains, segs,
    X_o, R_o, g_o, WQ_o, WKV_o, WO_o, TL_o, one_o, q_o, KV_o, P_o, heads_o, hidden_o, act_o, total, grads_o, PO, y_tmp, y_got,
    X, R, WQ, WKV, WO, TL, one, q, KV, probs_all, heads, hidden, ACT, G, GD, back, tw, tmp, got, gu_acc, dn_acc, grads, bias,
    wq32, wkv32, wo32, gate32, up32, dn32, wq16, wkv16, wo16, gd16, cos, sin, tail32, tail,
    ss, rs, ls,
):
    x, y, z, c = place()
    z_hi = z // 2
    slot = x * 2 + c
    net = Net(ss, rs, ls)
    kept = []
    keep = lambda src, dst: kept.append(net.local(src, dst))
    loads = [
        net.local(wqkv.at[:, pl.ds(pl.multiple_of(D + c * 512, 512), 512)], wkv32),
        net.local(wqkv.at[:, lanes(slot)], wq32),
        net.local(wout.at[:, lanes(slot)], wo32),
        net.local(wgu.at[:, :, lanes(x)], gate32),
        net.local(wgu.at[:, :, lanes(4 + x)], up32),
        net.local(wdn.at[:, pl.ds(pl.multiple_of(slot * SLICE, SLICE), SLICE), :], dn32),
    ]
    tables = [
        net.local(src.at[lanes(4 * h + y)], dst.at[pl.ds(128 * h, 128)])
        for src, dst in ((cos_t, cos), (sin_t, sin))
        for h in range(2)
    ]
    partner = dev(x, y, z + 2, c)
    over = dev(x, y, 3 - z, c)
    twin = dev(x, y, z, 1 - c)
    xr, xl = dev(x + 1, y, z, c), dev(x - 1, y, z, c)
    yr, yl = dev(x, y + 1, z, c), dev(x, y - 1, z, c)
    ys = [yr, yl, dev(x, y + 2, z, c)]
    net.greet(ys + [over, partner, twin, xr, xl])
    rows = [z_hi * 4, 4 - z_hi * 4]
    shards = [rows[0] + y, rows[1] + y]
    shards += [row + lax.rem(y + d, 4) for row in rows for d in (3, 1, 2)]
    half_rows = lanes(z_hi)
    kv_lanes = pl.ds(pl.multiple_of(c * 512, 512), 512)
    fan = lambda src, at: Fan(net, src, at, shards, over, ys)
    loads[0].wait()
    wkv16[...] = wkv32[...].astype(b16)
    kv_fan = fan(wkv16, lambda n: WKV.at[lanes(n), kv_lanes]).round()
    forwards = [net.send(wkv16, WKV.at[lanes(shards[0]), kv_lanes], twin)]
    own = [net.local(tok.at[z_hi], X.at[half_rows]), net.local(rl.at[z_hi], R.at[half_rows])]
    eye = lax.broadcasted_iota(jnp.int32, (128, 128), 0) == lax.broadcasted_iota(jnp.int32, (128, 128), 1)
    tail32[...] = jnp.zeros_like(tail32)
    tail32[0:6, :] = router[...]
    tail32[6:8, :] = gains[...]
    tail[...] = tail32[...].astype(b16)
    tl_fan = fan(tail, lambda n: TL.at[:, lanes(n)]).round()
    own += [
        net.local(wkv16, WKV.at[lanes(shards[0]), kv_lanes]),
        net.local(tail, TL.at[:, lanes(shards[0])]),
    ]

    place_k = lax.broadcasted_iota(jnp.int32, (128, D), 1)
    place_q = lax.broadcasted_iota(jnp.int32, (128, D), 0) + y * 128
    pick_row = lambda v: jnp.where(z_hi == 0, v[0:1], v[1:2]).astype(f32)
    seg_k = pick_row(segs[...])
    for h in range(2):
        seg_row = jnp.broadcast_to(pick_row(segs[:, lanes(4 * h + y)]), (128, 128))
        seg_q = jnp.sum(jnp.where(eye, seg_row, 0.0), axis=1, keepdims=True)
        fine = (place_q + 512 * h >= place_k) & (seg_q == seg_k)
        bias[128 * h : 128 * h + 128, :] = jnp.where(fine, 0.0, -1e30)

    ref = kv_fan.forward()
    forwards.append(net.send(ref, ref, twin))
    x_in = net.send(tok.at[1 - z_hi], X.at[half_rows], partner)
    tl_fan.forward()
    loads[1].wait()
    wq16[...] = wq32[...].astype(b16)
    q_fan = fan(wq16, lambda n: WQ.at[lanes(n), lanes(slot)])
    loads[2].wait()
    wo16[...] = wo32[...].astype(b16)
    o_fan = fan(wo16, lambda n: WO.at[lanes(n), lanes(slot)])
    more = [
        net.local(wq16, WQ.at[lanes(shards[0]), lanes(slot)]),
        net.local(wo16, WO.at[lanes(shards[0]), lanes(slot)]),
    ]
    r_in = net.send(rl.at[1 - z_hi], R.at[half_rows], partner)

    for copy in own + tables:
        copy.wait()
    for _ in tl_fan.arrivals():
        pass
    net.got(x_in)
    v = X[...].astype(f32)
    r = lax.rsqrt(jnp.mean(v * v, axis=-1, keepdims=True) + norm_epsilon)
    one[...] = (v * r * TL[6:7, :].astype(f32)).astype(b16)
    keep(X, X_o)
    keep(one, one_o)
    keep(TL, TL_o)

    for ref in kv_fan.arrivals():
        forwards.append(net.send(ref, ref, twin))
    for pieces in (q_fan, o_fan):
        pieces.round()
        pieces.forward()
    for copy in forwards:
        net.got(copy)
    cosine, sine = cos[...], sin[...]
    a = one[...]
    for t in range(4):
        out = dot(a, WKV[:, 256 * t : 256 * t + 256])
        for u in range(2):
            tile = out[:, 128 * u : 128 * u + 128]
            if t < 2:
                tile = tile * cosine + partner_lanes(tile) * sine
            KV[y, :, 256 * t + 128 * u : 256 * t + 128 * u + 128] = tile.astype(b16)
    kv_ring = Ring(net, lambda n, h: KV.at[n, pl.ds(h * 128, 128)], yr, yl, y)
    keep(WKV, WKV_o)

    for load in loads[3:]:
        load.wait()
    lane = lax.broadcasted_iota(jnp.int32, (128, 128), 1)
    mine_first = c == 0
    for part, src in enumerate((gate32, up32)):
        for b in range(3):
            one_e, two_e = src[2 * b], src[2 * b + 1]
            first = jnp.where(mine_first, one_e, pltpu.roll(one_e, SLICE, 1))
            second = jnp.where(mine_first, pltpu.roll(two_e, SLICE, 1), two_e)
            at = slice(128 * (3 * part + b), 128 * (3 * part + b) + 128)
            gd16[at, :] = jnp.where(lane < SLICE, first, second).astype(b16)
    gd16[2 * WIDE :, :] = dn32[...].reshape(WIDE, 128).astype(b16)
    gd_own = net.local(gd16, GD.at[shards[0]])
    gd_over = net.send(gd16, GD.at[shards[0]], over)
    g_in = net.send(cot.at[1 - z_hi], G.at[slot, half_rows], partner)
    g_own = net.local(cot.at[z_hi], G.at[slot, half_rows])
    for copy in more:
        copy.wait()

    rings, twins = [], []
    for pieces, whole in ((q_fan, WQ), (o_fan, WO)):
        for _ in pieces.arrivals():
            pass
        part = lambda n, h, whole=whole: whole.at[pl.ds(h * 512, 512), lanes(n * 2 + c)]
        rings.append(Ring(net, part, xr, xl, x))
        twins.append([net.send(whole.at[:, lanes(slot)], whole.at[:, lanes(slot)], twin)])
    kv_ring.relay()
    rings[0].relay()
    rings[1].relay()
    gd_own.wait()
    gd_part = lambda row: lambda n, h: GD.at[row + n, pl.ds(h * 576, 576)]
    gd_rings = [Ring(net, gd_part(rows[0]), yr, yl, y)]
    net.got(gd_over)
    gd_rings.append(Ring(net, gd_part(rows[1]), yr, yl, y))
    g_own.wait()
    net.got(g_in)
    g_ring = Ring(net, lambda n, h: G.at[n * 2 + c, pl.ds(h * 128, 128)], xr, xl, x)
    g_twin = net.send(G.at[slot], G.at[slot], twin)
    keep(G.at[slot], g_o)

    def share(n, whole):
        rings[n].done()
        for d in range(1, 4):
            tile = whole.at[:, lanes(lax.rem(x + d, 4) * 2 + c)]
            twins[n].append(net.send(tile, tile, twin))

    share(0, WQ)
    for copy in twins[0]:
        net.got(copy)
    for t in range(4):
        out = dot(a, WQ[:, 256 * t : 256 * t + 256])
        for u in range(2):
            tile = out[:, 128 * u : 128 * u + 128]
            tile = tile * cosine + partner_lanes(tile) * sine
            q[:, 256 * t + 128 * u : 256 * t + 128 * u + 128] = (tile * 0.125).astype(b16)
    keep(q, q_o)
    keep(WQ, WQ_o)
    kv_ring.done()
    keep(KV, KV_o)

    low_bias = jnp.concatenate([bias[:128, :512]] * 2, axis=0)
    high_bias = jnp.concatenate([bias[128:, :]] * 2, axis=0)

    def attend(pair, carry):
        cols, vcols = lanes(pair), lanes(4 + pair)
        keys = [KV[:, :128, cols].reshape(512, 128), KV[:, 128:, cols].reshape(512, 128)]
        vals = [KV[:, :128, vcols].reshape(512, 128), KV[:, 128:, vcols].reshape(512, 128)]
        keys_all = jnp.concatenate(keys, axis=0)
        vals_all = jnp.concatenate(vals, axis=0)
        for half in range(2):
            cols = lanes(2 * pair + half)
            low, high = spread(q[:, cols].astype(f32), half)
            outs = []
            for qq, kk, vv, bb, at_p in (
                (low, keys[0], vals[0], low_bias, slice(0, 512)),
                (high, keys_all, vals_all, high_bias, slice(512, 1536)),
            ):
                s = dot_t(qq, kk) + bb
                top = jnp.max(s, axis=-1, keepdims=True)
                e = jnp.exp(s - top)
                probs = (e * (1.0 / jnp.sum(e, axis=-1, keepdims=True))).astype(b16)
                probs_all[2 * pair + half, :, at_p] = probs
                outs.append(dot(probs, vv))
            heads[:, cols] = collect(outs[0], outs[1], half).astype(b16)
        return carry

    for m in range(2):
        lax.fori_loop(2 * m, 2 * m + 2, attend, 0)
        keep(probs_all.at[pl.ds(4 * m, 4)], P_o.at[pl.ds(4 * m, 4)])
        if m == 0:
            share(1, WO)
            g_ring.relay()
            gd_rings[0].relay()
    gd_rings[1].relay()
    keep(heads, heads_o)

    for copy in twins[1]:
        net.got(copy)
    keep(WO, WO_o)
    all_heads = heads[...]
    for t in range(4):
        cols = slice(256 * t, 256 * t + 256)
        hidden[:, cols] = X[:, cols].astype(f32) + dot(all_heads, WO[:, cols])
    h = hidden[...]
    r = lax.rsqrt(jnp.mean(h * h, axis=-1, keepdims=True) + norm_epsilon)
    a = (h * r * TL[7:8, :].astype(f32)).astype(b16)
    ACT[slot, :, :D] = a
    logits = dot_t(a, router_rows(TL[...]))
    net.got(r_in)
    routes = R[...]
    hots = [one_hot(routes, k) for k in range(TOPK)]
    picked = [jnp.sum(hot * logits, axis=-1, keepdims=True) for hot in hots]
    top = jnp.maximum(picked[0], picked[1])
    powers = [jnp.exp(v - top) for v in picked]
    power = powers[0] + powers[1]
    mixing = hots[0] * (powers[0] / power) + hots[1] * (powers[1] / power)
    big = mixing.astype(b16).astype(f32)
    ACT[slot, :, D:] = (big + pltpu.roll(mixing - big, 16, 1)).astype(b16)
    chips = {d: lax.rem(x + d, 4) for d in range(4)}
    mine = {d: chips[d] * 2 + c for d in range(4)}
    other = {d: chips[d] * 2 + 1 - c for d in range(4)}
    lo, hi = pl.ds(0, 128), pl.ds(128, 128)
    ins, outs = pl.ds(0, D + 128), pl.ds(D + 128, D)
    before, across, after = chips[3], chips[2], chips[1]
    home_block = ACT.at[slot]
    swap = net.send(home_block, home_block, twin)
    a1 = net.send(ACT.at[slot, lo], ACT.at[slot, lo], xr)
    b1 = net.send(ACT.at[slot, hi], ACT.at[slot, hi], xl)
    gu_acc[...] = jnp.zeros_like(gu_acc)
    dn_acc[...] = jnp.zeros_like(dn_acc)
    row = lax.broadcasted_iota(jnp.int32, (128, WIDE), 0)
    lane = lax.broadcasted_iota(jnp.int32, (128, WIDE), 1)
    pick = ((row % 16 == lane // SLICE) & (row < 32)).astype(b16)

    def compute(parts):
        weights = jnp.concatenate(
            [GD[:, 128 * b : 128 * b + 128].reshape(D, 128) for b in range(6)], axis=1
        )
        down_w = jnp.concatenate([GD[n, 2 * WIDE :] for n in range(8)], axis=1)
        both = lambda ref, cols: jnp.concatenate([ref[n, at, cols] for n, at in parts], axis=0)
        a = both(ACT, slice(0, D))
        mix = dot(both(ACT, slice(D, D + 128)), pick)
        gt = both(G, slice(0, D))
        h = dot(a, weights)
        gate, up = h[:, :WIDE], h[:, WIDE:]
        gw = dot_t(gt, down_w)
        s = 1.0 / (1.0 + jnp.exp(-gate))
        silu = gate * s
        inner = silu * up
        scaled = (inner * mix).astype(b16)
        gi = gw * mix
        ggu = jnp.concatenate(
            [(gi * up * s * (1.0 + gate * (1.0 - s))).astype(b16), (gi * silu).astype(b16)], axis=1
        )
        down = dot_t(ggu, weights).astype(b16)
        dots = dot_t((inner * gw).astype(b16), pick).astype(b16)
        terms = dot(scaled, down_w).astype(b16)
        for i, (n, at) in enumerate(parts):
            rows = slice(128 * i, 128 * i + 128)
            back[n, at, :D] = down[rows]
            back[n, at, D : D + 128] = dots[rows]
            back[n, at, D + 128 :] = terms[rows]
        gu_acc[...] += t_dot(a, ggu)
        dn_acc[...] += t_dot(scaled, gt)

    def add(dst, one, two):
        add_rows(dst, one, two, dst.shape[0], 16)

    def units(chip, offset, pieces):
        first = net.count
        sent = [net.planned(back.at[other[d], at], tw.at[chips[d], at], twin) for d, at in pieces]

        def one_unit(j, carry):
            n, at = chip(j), pl.ds(pl.multiple_of(offset(j), 128), 128)
            compute([(n * 2 + c, at), (n * 2 + 1 - c, at)])
            net.describe(first + j, back.at[n * 2 + 1 - c, at], tw.at[n, at], twin).start()
            return carry

        lax.fori_loop(0, 2, one_unit, 0)
        return sent

    def settle(d, at, sent):
        net.got(sent)
        add(tw.at[chips[d], at], tw.at[chips[d], at], back.at[mine[d], at])
        keep(tw.at[chips[d], at, outs], PO.at[chips[d], at])

    def forward(d, at, arrive):
        net.got(arrive)
        block = ACT.at[mine[d], at]
        return net.send(block, block, twin)

    keep(hidden, hidden_o)
    keep(ACT.at[slot], act_o)
    keep(R, R_o)
    for pieces in gd_rings:
        pieces.done()
    net.got(swap)
    net.got(g_twin)

    def own_chip(j, carry):
        n = x * 2 + lax.rem(c + j, 2)
        compute([(n, lo), (n, hi)])
        return carry

    lax.fori_loop(0, 2, own_chip, 0)
    home = net.send(back.at[other[0]], tw.at[x], twin)
    net.got(a1)
    a3 = net.send(ACT.at[mine[3], lo], ACT.at[mine[3], lo], xr)
    net.got(b1)
    b3 = net.send(ACT.at[mine[1], hi], ACT.at[mine[1], hi], xl)
    a2 = net.send(ACT.at[slot, hi], ACT.at[slot, hi], xr)
    b2 = net.send(ACT.at[slot, lo], ACT.at[slot, lo], xl)
    f1, f2 = (net.send(ACT.at[mine[d], at], ACT.at[mine[d], at], twin) for d, at in ((3, lo), (1, hi)))
    g_ring.done()
    g_far = [net.send(G.at[mine[d]], G.at[mine[d]], twin) for d in (3, 1, 2)]
    for copy in g_far:
        net.got(copy)
    for copy in (f1, f2):
        net.got(copy)
    ends_of = lambda j: lax.rem(x + 3 - 2 * j, 4)
    u1, u2 = units(ends_of, lambda j: 128 * j, [(3, lo), (1, hi)])
    f3 = forward(2, lo, a3)
    f4 = forward(2, hi, b3)
    settle(3, lo, u1)
    last = [net.send(tw.at[before, lo, ins], got.at[1, lo], xl)]
    settle(1, hi, u2)
    last.append(net.send(tw.at[after, hi, ins], got.at[0, hi], xr))
    for copy in (f3, f4):
        net.got(copy)
    u3, u4 = units(lambda j: across, lambda j: 128 * j, [(2, lo), (2, hi)])
    f5 = forward(3, hi, a2)
    f6 = forward(1, lo, b2)
    settle(2, lo, u3)
    s1 = net.send(tw.at[across, lo, ins], tmp.at[0], xr)
    settle(2, hi, u4)
    s2 = net.send(tw.at[across, hi, ins], tmp.at[1], xl)
    for copy in (f5, f6):
        net.got(copy)
    u5, u6 = units(ends_of, lambda j: 128 - 128 * j, [(3, hi), (1, lo)])
    net.got(home)
    add(tw.at[x], tw.at[x], back.at[mine[0]])
    keep(tw.at[x, :, outs], PO.at[x])
    for n in range(8):
        at = slice(128 * n, 128 * n + 128)
        for b in range(6):
            grads[n, 128 * b : 128 * b + 128] = gu_acc[at, 128 * b : 128 * b + 128].astype(b16)
        for b in range(3):
            rows = slice(128 * (6 + b), 128 * (6 + b) + 128)
            grads[n, rows] = dn_acc[128 * b : 128 * b + 128, at].astype(b16)
    keep(grads, grads_o)
    for n in range(2):
        Scatter(net, lambda k, n=n: grads.at[n * 4 + k], y_tmp.at[n], y_got.at[n], yr, yl, y, 1152, 64)
    settle(3, hi, u5)
    settle(1, lo, u6)
    net.got(s1)
    add(tmp.at[0], tmp.at[0], tw.at[after, lo, ins])
    last.append(net.send(tmp.at[0], got.at[0, lo], xr))
    net.got(s2)
    add(tmp.at[1], tmp.at[1], tw.at[before, hi, ins])
    last.append(net.send(tmp.at[1], got.at[1, hi], xl))
    for copy in last:
        net.got(copy)

    def body(i, carry):
        at = pl.ds(pl.multiple_of(i * 16, 16), 16)
        total[at] = tw[x, at, : D + 128].astype(f32) + got[0, at].astype(f32) + got[1, at].astype(f32)
        return carry

    lax.fori_loop(0, ROWS // 16, body, 0)
    for copy in kept:
        copy.wait()
    net.finish()


def front(*arrays):
    V = pltpu.VMEM
    wide = D + 128
    return pl.pallas_call(
        front_kernel,
        out_shape=(
            shape((ROWS, D), b16),
            shape((ROWS, 128), jnp.int32),
            shape((ROWS, D), b16),
            shape((D, D), b16),
            shape((D, D), b16),
            shape((D, D), b16),
            shape((16, D), b16),
            shape((ROWS, D), b16),
            shape((ROWS, D), b16),
            shape((4, ROWS, D), b16),
            shape((8, ROWS, 1536), b16),
            shape((ROWS, D), b16),
            shape((ROWS, D), f32),
            shape((ROWS, D + 128), b16),
            shape((ROWS, wide), f32),
            shape((8, 9 * 128, 128), b16),
            shape((4, ROWS, D), b16),
            shape((2, 2, 576, 128), b16),
            shape((2, 2, 1152, 128), b16),
        ),
        in_specs=[ANY] * 9 + [VMEM] * 3,
        out_specs=(ANY,) * 14 + (VMEM,) + (ANY,) * 4,
        scratch_shapes=[
            V((ROWS, D), b16),
            V((ROWS, 128), jnp.int32),
            V((D, D), b16),
            V((D, D), b16),
            V((D, D), b16),
            V((16, D), b16),
            V((ROWS, D), b16),
            V((ROWS, D), b16),
            V((4, ROWS, D), b16),
            V((8, ROWS, 1536), b16),
            V((ROWS, D), b16),
            V((ROWS, D), f32),
            V((8, ROWS, wide), b16),
            V((8, ROWS, D), b16),
            V((8, 3 * WIDE, 128), b16),
            V((8, ROWS, wide + D), b16),
            V((4, ROWS, wide + D), b16),
            V((2, ROWS // 2, wide), b16),
            V((2, ROWS, wide), b16),
            V((D, 2 * WIDE), f32),
            V((WIDE, D), f32),
            V((8, 9 * 128, 128), b16),
            V((ROWS, D), f32),
            V((128, 128), f32),
            V((128, 512), f32),
            V((128, 128), f32),
            V((EXPERTS, 128, 128), f32),
            V((EXPERTS, 128, 128), f32),
            V((EXPERTS, SLICE, 128), f32),
            V((128, 128), b16),
            V((128, 512), b16),
            V((128, 128), b16),
            V((3 * WIDE, 128), b16),
            V((ROWS, 128), f32),
            V((ROWS, 128), f32),
            V((16, 128), f32),
            V((16, 128), b16),
        ]
        + sems(160, 64),
        compiler_params=params(0, 62),
        name="front",
    )(*arrays)


def back_kernel(
    total_i, hidden_i, act_i, g_i, TL_i, R_i, heads_i, WO_i, X_i, one_i, q_i, KV_i, P_i, WQ_i, WKV_i,
    grads_i, PO, y_tmp_i, y_got_i, cos_t, sin_t,
    OUT, GIN, ALLM, ALL, SM,
    total, hidden, act, g, TL, R, heads, heads_t, WO, X, one, one_t, q, KV, P, WQ, WKV, gr, po, po_tmp, po_got,
    o_t, o_w, o_tmp, o_got, q_t, q_w, q_tmp, q_got, k_t, k_w, k_tmp, k_got,
    dkv, kv_tmp, kv_got, gh, ghl, ghi, gp, gin, gin_low, gin_got, ob, cos, sin,
    y_tmp, y_got, z_got, o_mine, o_in, q_mine, q_in, oq, oq_in, k_mine, k_in, small, s_twin, s_x, s_y, s_z,
    ss, rs, ls,
):
    x, y, z, c = place()
    z_hi, z_lo = z // 2, lax.rem(z, 2)
    slot = x * 2 + c
    net = Net(ss, rs, ls)
    kept = []
    twin = dev(x, y, z, 1 - c)
    xs = [dev(x + d, y, z, c) for d in (1, 3, 2)]
    ys = [dev(x, y + d, z, c) for d in (1, 3, 2)]
    zs = [dev(x, y, z + d, c) for d in (1, 3, 2)]
    flip = z + 1 - 2 * z_lo
    others = [dev(x + d, y, flip, c) for d in (1, 3, 2)]
    plane = [(dy, dz) for dz in range(4) for dy in range(4) if dy or dz]
    (xr, xl, x2), (yr, yl, y2), (zr, zl, z2) = xs, ys, zs
    net.call([twin] + xs + others + [dev(x, y + dy, z + dz, c) for dy, dz in plane])
    first = [
        net.local(*pair)
        for pair in (
            (total_i, total), (hidden_i, hidden), (act_i, act), (TL_i, TL), (R_i, R),
            (g_i, g), (WO_i, WO),
        )
    ]
    grad_load = [net.local(grads_i, gr), net.local(y_tmp_i, y_tmp)]
    for n in range(2):
        at = pl.ds(576 * (1 - n), 576)
        grad_load.append(net.local(y_got_i.at[:, n, at], y_got.at[:, n, at]))
    po_load = net.local(PO, po)
    for copy in first:
        copy.wait()
    second = [
        net.local(*pair)
        for pair in ((KV_i, KV), (q_i, q), (P_i, P), (heads_i, heads), (one_i, one), (X_i, X), (WQ_i, WQ), (WKV_i, WKV))
    ]
    second += [
        net.local(src.at[lanes(4 * h + y)], dst.at[pl.ds(128 * h, 128)])
        for src, dst in ((cos_t, cos), (sin_t, sin))
        for h in range(2)
    ]

    h = hidden[...]
    a = act[:, :D]
    mix = act[:, D:].astype(f32)
    lane = lax.broadcasted_iota(jnp.int32, (ROWS, 128), 1)
    mixing = jnp.where(lane < 16, mix + pltpu.roll(mix, 112, 1), 0.0)
    dg = total[:, D:]
    routes = R[...]
    hots = [one_hot(routes, k) for k in range(TOPK)]
    probs = [jnp.sum(hot * mixing, axis=-1, keepdims=True) for hot in hots]
    dgs = [jnp.sum(hot * dg, axis=-1, keepdims=True) for hot in hots]
    mean = probs[0] * dgs[0] + probs[1] * dgs[1]
    grad_logits = sum(hot * (p * (d - mean)) for hot, p, d in zip(hots, probs, dgs)).astype(b16)
    ga = total[:, :D] + dot(grad_logits, router_rows(TL[...]))
    small[0:6, :] = t_dot(grad_logits, a)[0:6, :]
    r = lax.rsqrt(jnp.mean(h * h, axis=-1, keepdims=True) + norm_epsilon)
    u = ga * TL[7:8, :].astype(f32)
    small[6:7, :] = jnp.sum(ga * h * r, axis=0, keepdims=True)
    gh[...] = g[...].astype(f32) + r * (u - h * (r * r * jnp.mean(u * h, axis=-1, keepdims=True)))
    ghl[...] = gh[...].astype(b16)

    net.answer()
    for copy in grad_load:
        copy.wait()
    y_rings = [
        Scatter(net, lambda n, h=h: gr.at[h * 4 + n], y_tmp.at[h], y_got.at[h], yr, yl, y, 1152, 64, begin=False)
        for h in range(2)
    ]
    for ring in y_rings:
        ring.relay()
    po_load.wait()
    out_ring = Scatter(net, lambda n: po.at[n], po_tmp, po_got, xr, xl, x, ROWS, 16)

    def columns(src, dst, first=0):
        return [net.send(src.at[:, lanes(first + 2 * n + 1 - c)], dst.at[n], twin) for n in range(4)]

    o_sent = columns(ghl, o_t)
    lefts = [net.send(heads_i, heads_t, twin), net.send(one_i, one_t, twin)]
    ghi[...] = dot_t(ghl[...], WO[...]).astype(b16)

    def weight_grad(left, left_t, right, first, right_t, sent, store):
        for copy in sent:
            net.got(copy)
        for m in range(2):
            own = jnp.concatenate([right[:, lanes(first + 2 * n + c)] for n in (2 * m, 2 * m + 1)], axis=1)
            far = jnp.concatenate([right_t[2 * m], right_t[2 * m + 1]], axis=1)
            piece = (t_dot(left[...], own) + t_dot(left_t[...], far)).astype(b16)
            for i in range(2):
                store(2 * m + i, piece[:, 128 * i : 128 * i + 128])

    def store_o(n, tile):
        o_w[n] = tile

    def store_k(n, tile):
        k_w[n] = tile

    def store_q(n, tile):
        for shard in range(8):
            row = 256 * n + 128 * (shard // 4)
            q_w[shard % 4, row : row + 128] = tile[128 * shard : 128 * shard + 128]

    for copy in second:
        copy.wait()
    cosine, sine = cos[...], sin[...]

    def pair(n, carry):
        cols, vcols = lanes(n), lanes(4 + n)
        keys = [KV[:, :128, cols].reshape(512, 128), KV[:, 128:, cols].reshape(512, 128)]
        vals = [KV[:, :128, vcols].reshape(512, 128), KV[:, 128:, vcols].reshape(512, 128)]
        keys_all = jnp.concatenate(keys, axis=0)
        vals_all = jnp.concatenate(vals, axis=0)
        sums = None
        for half in range(2):
            at = lanes(2 * n + half)
            q_low, q_high = spread(q[:, at].astype(f32), half)
            do_low, do_high = spread(ghi[:, at].astype(f32), half)
            outs, terms = [], []
            for qq, dd, kk, vv, at_p in (
                (q_low, do_low, keys[0], vals[0], slice(0, 512)),
                (q_high, do_high, keys_all, vals_all, slice(512, 1536)),
            ):
                pr = P[2 * n + half, :, at_p]
                dp = dot_t(dd, vv)
                pf = pr.astype(f32)
                prod = pf * dp
                ds = (prod - pf * jnp.sum(prod, axis=-1, keepdims=True)).astype(b16)
                outs.append(dot(ds, kk) * 0.125)
                terms.append((t_dot(ds, qq), t_dot(pr, dd)))
            tile = collect(outs[0], outs[1], half)
            gp[:, at] = (tile * cosine - partner_lanes(tile) * sine).astype(b16)
            sums = terms if half == 0 else [(i + k, j + m) for (i, j), (k, m) in zip(sums, terms)]
        for part in range(2):
            lows, whole = sums[0][part], sums[1][part]
            where = lanes(2 * part + lax.rem(n, 2))
            dkv[n // 2, :, :128, where] = (lows + whole[:512]).reshape(4, 128, 128).astype(b16)
            dkv[n // 2, :, 128:, where] = whole[512:].reshape(4, 128, 128).astype(b16)
        return carry

    def keys_home(n):
        return Scatter(net, lambda k: dkv.at[n, k], kv_tmp.at[n], kv_got.at[n], yr, yl, y, ROWS, 32)

    lax.fori_loop(0, 2, pair, 0)
    kv_rings = [keys_home(0)]
    for n, ring in enumerate(y_rings):
        ring.done()
        ring.settle(gr.at[n * 4 + y], 1152, 64)

    def piece(zz):
        return gr.at[(zz // 2) * 4 + y, pl.ds(pl.multiple_of(lax.rem(zz, 2) * 576, 576), 576)]

    z_in = [net.send(piece(lax.rem(z + d, 4)), z_got.at[i], zs[i]) for i, d in enumerate((1, 3, 2))]
    out_ring.relay()
    net.got(lefts[0])
    weight_grad(heads, heads_t, ghl, 0, o_t, o_sent, store_o)
    o_ring = Scatter(net, lambda n: o_w.at[n], o_tmp, o_got, xr, xl, x, 1024, 64)
    lax.fori_loop(2, 4, pair, 0)
    kv_rings.append(keys_home(1))
    kv_rings[0].relay()
    q_sent = columns(gp, q_t)
    for copy in z_in:
        net.got(copy)
    base = pl.multiple_of(z_lo * 576, 576)
    for i in range(9):
        at = slice(64 * i, 64 * i + 64)
        here = pl.ds(pl.multiple_of(base + 64 * i, 64), 64)
        v = gr[z_hi * 4 + y, here].astype(f32)
        for n in range(3):
            v = v + z_got[n, at].astype(f32)
        z_got[0, at] = v.astype(b16)
    half_m = ALLM.at[slot, pl.ds(base, 576)]
    own_m = net.local(z_got.at[0], half_m)
    hop = net.send(z_got.at[0], half_m, dev(x, y, flip, c))

    o_ring.relay()
    net.got(lefts[1])
    weight_grad(one, one_t, gp, 0, q_t, q_sent, store_q)
    own_m.wait()
    net.got(hop)
    block = ALLM.at[slot]
    net.send(block, block, twin)
    m_ring = Ring(net, lambda n, h: ALLM.at[n * 2 + c, pl.ds(h * 576, 576)], xr, xl, x)
    kv_rings[1].relay()
    q_ring = Scatter(net, lambda n: q_w.at[n], q_tmp, q_got, yr, yl, y, 1024, 64)
    ga = dot_t(gp[:, :D], WQ[...])
    out_ring.done()
    ob[...] = (hidden[...] + out_ring.term(slice(None))).astype(b16)
    rows_of = lambda n: pl.ds(pl.multiple_of(n * 128, 128), 128)
    net.send(ob.at[rows_of(1 - z_hi)], OUT.at[z_hi], z2)
    kept.append(net.local(ob.at[rows_of(z_hi)], OUT.at[z_hi]))

    for n in range(2):
        kv_rings[n].done()
        for part in range(2):
            for i in range(2):
                src = slice(256 * part + 128 * i, 256 * part + 128 * i + 128)
                tile = dkv[n, y, :, src].astype(f32)
                tile = tile + kv_got[n, 0, :, src].astype(f32) + kv_got[n, 1, :, src].astype(f32)
                if part == 0:
                    tile = tile * cosine - partner_lanes(tile) * sine
                to = D + 512 * part + 256 * n + 128 * i
                gp[:, to : to + 128] = tile.astype(b16)
    k_sent = columns(gp, k_t, 8)
    ga = ga + dot_t(gp[:, D:], WKV[...])
    weight_grad(one, one_t, gp, 8, k_t, k_sent, store_k)
    k_ring = Scatter(net, lambda n: k_w.at[n], k_tmp, k_got, xr, xl, x, 1024, 64)
    v = X[...].astype(f32)
    r = lax.rsqrt(jnp.mean(v * v, axis=-1, keepdims=True) + norm_epsilon)
    u = ga * TL[6:7, :].astype(f32)
    small[7:8, :] = jnp.sum(ga * v * r, axis=0, keepdims=True)
    sm = net.send(small, s_twin, twin)
    gin[...] = gh[...] + r * (u - v * (r * r * jnp.mean(u * v, axis=-1, keepdims=True)))
    gin_low[...] = gin[rows_of(1 - z_hi)].astype(b16)
    swap = net.send(gin_low, gin_got, z2)
    gin_kept = net.local(gin.at[rows_of(z_hi)], GIN.at[z_hi])
    m_ring.relay()
    q_ring.relay()
    o_ring.done()
    for n in range(8):
        o_mine[n] = o_ring.term(slice(128 * n, 128 * n + 128)).astype(b16)
    o_sent = [
        net.send(o_mine.at[h * 4 + lax.rem(y + d, 4)], o_in.at[h, i], ys[i])
        for h in range(2)
        for i, d in enumerate((1, 3, 2))
    ]
    net.got(sm)
    s_twin[...] += small[...]
    sx = [net.send(s_twin, s_x.at[i], p) for i, p in enumerate(xs)]
    k_ring.relay()
    q_ring.done()
    for n in range(4):
        q_mine[n] = q_ring.term(slice(256 * n, 256 * n + 256)).astype(b16)
    q_sent = [net.send(q_mine.at[lax.rem(x + d, 4)], q_in.at[i], xs[i]) for i, d in enumerate((1, 3, 2))]
    for copy in sx:
        net.got(copy)
    s_y[0] = s_twin[...] + s_x[0] + s_x[1] + s_x[2]
    sy = [net.send(s_y.at[0], s_y.at[1 + i], p) for i, p in enumerate(ys)]
    for copy in o_sent:
        net.got(copy)
    net.got(swap)
    gin_kept.wait()
    gin[rows_of(z_hi)] = gin_got[...].astype(f32)
    kept.append(net.local(gin.at[rows_of(z_hi)], GIN.at[1 - z_hi]))
    k_ring.done()
    for n in range(8):
        k_mine[n] = k_ring.term(slice(128 * n, 128 * n + 128)).astype(b16)

    def k_piece(dy, dz):
        zz = lax.rem(z + dz, 4)
        half = pl.ds(pl.multiple_of(lax.rem(zz, 2) * 64, 64), 64)
        return k_mine.at[(zz // 2) * 4 + lax.rem(y + dy, 4), half]

    k_sent = [
        net.send(k_piece(dy, dz), k_in.at[i], dev(x, y + dy, z + dz, c)) for i, (dy, dz) in enumerate(plane)
    ]
    for copy in sy:
        net.got(copy)
    s_z[0] = s_y[0] + s_y[1] + s_y[2] + s_y[3]
    sz = [net.send(s_z.at[0], s_z.at[1 + i], p) for i, p in enumerate(zs)]
    for copy in q_sent:
        net.got(copy)
    for h in range(2):
        o_sum = o_mine[h * 4 + y].astype(f32)
        q_sum = q_mine[x, 128 * h : 128 * h + 128].astype(f32)
        for i in range(3):
            o_sum = o_sum + o_in[h, i].astype(f32)
            q_sum = q_sum + q_in[i, 128 * h : 128 * h + 128].astype(f32)
        for low in range(2):
            oq[2 * h + low, 0:64] = o_sum[64 * low : 64 * low + 64].astype(b16)
            oq[2 * h + low, 64:128] = q_sum[64 * low : 64 * low + 64].astype(b16)
    oq_sent = [net.send(oq.at[lax.rem(z + d, 4)], oq_in.at[i], zs[i]) for i, d in enumerate((1, 3, 2))]
    m_ring.done()
    for d in range(1, 4):
        block = ALLM.at[lax.rem(x + d, 4) * 2 + c]
        net.send(block, block, twin)
    for copy in oq_sent + k_sent:
        net.got(copy)
    late_half = lambda chip, low: ALL.at[chip * 2 + c, pl.ds(pl.multiple_of(low * 192, 192), 192)]
    oq_sum = oq[z].astype(f32)
    for i in range(3):
        oq_sum = oq_sum + oq_in[i].astype(f32)
    half = pl.ds(pl.multiple_of(z_lo * 64, 64), 64)
    k_sum = k_mine[z_hi * 4 + y, half].astype(f32)
    for i in range(15):
        k_sum = k_sum + k_in[i].astype(f32)
    base = pl.multiple_of(z_lo * 192, 192)
    ALL[slot, pl.ds(base, 128)] = oq_sum.astype(b16)
    ALL[slot, pl.ds(pl.multiple_of(base + 128, 64), 64)] = k_sum.astype(b16)
    piece_here = late_half(x, z_lo)
    ends = [net.send(piece_here, piece_here, p) for p in xs + [dev(x, y, flip, c)] + others]
    net.send(piece_here, piece_here, twin)
    for copy in sz:
        net.got(copy)
    here = lanes(z_hi * 4 + y)
    SM[...] = s_z[0, :, here] + s_z[1, :, here] + s_z[2, :, here] + s_z[3, :, here]
    came = [(lax.rem(x + d, 4), z_lo) for d in (3, 1, 2)] + [(x, 1 - z_lo)]
    came += [(lax.rem(x + d, 4), 1 - z_lo) for d in (3, 1, 2)]
    for copy, (chip, low) in zip(ends, came):
        net.got(copy)
        block = late_half(chip, low)
        net.send(block, block, twin)
    for copy in kept:
        copy.wait()
    net.finish()


def back(*arrays):
    V = pltpu.VMEM
    wide = D + 128
    return pl.pallas_call(
        back_kernel,
        out_shape=(
            shape((2, 128, D), b16),
            shape((2, 128, D), f32),
            shape((8, 1152, 128), b16),
            shape((8, 384, 128), b16),
            shape((8, 128), f32),
        ),
        in_specs=[ANY] * 21,
        out_specs=(ANY, ANY, ANY, VMEM, VMEM),
        scratch_shapes=[
            V((ROWS, wide), f32),
            V((ROWS, D), f32),
            V((ROWS, wide), b16),
            V((ROWS, D), b16),
            V((16, D), b16),
            V((ROWS, 128), jnp.int32),
            V((ROWS, D), b16),
            V((ROWS, D), b16),
            V((D, D), b16),
            V((ROWS, D), b16),
            V((ROWS, D), b16),
            V((ROWS, D), b16),
            V((ROWS, D), b16),
            V((4, ROWS, D), b16),
            V((8, ROWS, 1536), b16),
            V((D, D), b16),
            V((D, D), b16),
            V((8, 1152, 128), b16),
            V((4, ROWS, D), b16),
            V((2, ROWS // 2, D), b16),
            V((2, ROWS, D), b16),
        ]
        + [
            V((4, ROWS, 128), b16),
            V((4, D, 128), b16),
            V((2, D // 2, 128), b16),
            V((2, D, 128), b16),
        ]
        * 3
        + [
            V((2, 4, ROWS, 512), b16),
            V((2, 2, ROWS // 2, 512), b16),
            V((2, 2, ROWS, 512), b16),
            V((ROWS, D), f32),
            V((ROWS, D), b16),
            V((ROWS, D), b16),
            V((ROWS, 2 * D), b16),
            V((ROWS, D), f32),
            V((128, D), b16),
            V((128, D), b16),
            V((ROWS, D), b16),
            V((ROWS, 128), f32),
            V((ROWS, 128), f32),
            V((2, 2, 576, 128), b16),
            V((2, 2, 1152, 128), b16),
            V((3, 576, 128), b16),
            V((8, 128, 128), b16),
            V((2, 3, 128, 128), b16),
            V((4, 256, 128), b16),
            V((3, 256, 128), b16),
            V((4, 128, 128), b16),
            V((3, 128, 128), b16),
            V((8, 128, 128), b16),
            V((15, 64, 128), b16),
            V((8, D), f32),
            V((8, D), f32),
            V((3, 8, D), f32),
            V((4, 8, D), f32),
            V((4, 8, D), f32),
        ]
        + sems(128, 40),
        compiler_params=params(3, 60),
        name="back",
    )(*arrays)


def rotary():
    freqs = np.float32(10000.0) ** (-np.arange(HD // 2, dtype=np.float32) * np.float32(2.0) / np.float32(HD))
    angles = np.arange(D, dtype=np.float32)[:, None] * freqs[None, :]
    cos, sin = np.cos(angles), np.sin(angles)
    return np.concatenate([cos] * 4, axis=1), np.concatenate([-sin, sin] * 2, axis=1)


def learning_rates():
    return (D ** (-0.5), 8.0 * D ** (-0.5), D ** (-0.5), 2.0 * FF ** (-0.5), 0.5 * D ** (-0.5), 0.5)


def adamw(weight, gradient, moment, square, step_rate, decay_rate):
    moment_new = beta_one * moment + (1.0 - beta_one) * gradient
    square_new = beta_two * square + (1.0 - beta_two) * gradient * gradient
    corrected = moment_new / (1.0 - beta_one**STEP)
    spread_by = jnp.sqrt(square_new / (1.0 - beta_two**STEP)) + adam_epsilon
    updated = weight - step_rate * (corrected / spread_by + decay_rate * weight)
    return [moment_new, square_new, updated]


def update_kernel(*refs):
    moe_i, late_i, out_i, gin_i, sums = refs[:5]
    ins, small_ins, outs, small_outs = refs[5:17], refs[17:23], refs[25:37], refs[37:43]
    moe, late, bufs, passing, sem = refs[43], refs[44], refs[45:57], refs[57:59], refs[59]
    rates = learning_rates()
    lane = lax.broadcasted_iota(jnp.int32, (128, 128), 1)
    count = 0

    def copy(src, dst):
        nonlocal count
        made = pltpu.make_async_copy(src, dst, sem.at[count])
        made.start()
        count += 1
        return made

    grads = [copy(moe_i, moe), copy(late_i, late)]
    every = slice(None)
    chunks = [(0, pl.ds(2 * b, 2)) for b in range(3)] + [(1, pl.ds(2 * b, 2)) for b in range(3)]
    chunks += [(2, (every, pl.ds(1024 * p, 1024))) for p in range(2)] + [(3, every)]
    loads = [
        [copy(ins[3 * n + i].at[at], bufs[3 * n + i].at[at]) for i in range(3)] for n, at in chunks
    ]
    through = [copy(src, dst) for src, dst in zip((out_i, gin_i), passing)]
    for n, (grad, rate, decay) in enumerate(
        (
            (sums[0:6, :], rates[4], 0.1),
            (jnp.concatenate([sums[7:8, :], sums[6:7, :]], axis=0), rates[5], 0.0),
        )
    ):
        w, m, v = (ref[...] for ref in small_ins[3 * n : 3 * n + 3])
        for ref, value in zip(small_outs[3 * n : 3 * n + 3], adamw(w, grad, m, v, rate, decay)):
            ref[...] = value
    for load in grads:
        load.wait()
    stores = []

    def apply(n, at, grad, rate):
        w, m, v = bufs[3 * n : 3 * n + 3]
        m[at], v[at], w[at] = adamw(w[at], grad, m[at], v[at], rate, 0.1)

    for step, (n, at) in enumerate(chunks):
        for load in loads[step]:
            load.wait()
        if n == 0:
            b = step

            def tiles(t, carry, b=b):
                for part in range(2):
                    rows = slice(128 * (3 * part + b), 128 * (3 * part + b) + 128)
                    one, two = moe[2 * t, rows].astype(f32), moe[2 * t + 1, rows].astype(f32)
                    cols = lanes(4 * part + t)
                    first = jnp.where(lane < SLICE, one, pltpu.roll(two, SLICE, 1))
                    second = jnp.where(lane < SLICE, pltpu.roll(one, SLICE, 1), two)
                    apply(0, (2 * b, every, cols), first, rates[2])
                    apply(0, (2 * b + 1, every, cols), second, rates[2])
                return carry

            lax.fori_loop(0, 4, tiles, 0)
        elif n == 1:
            b = step - 3

            def tiles(k, carry, b=b):
                for e in range(2):
                    row = 128 * (6 + b) + SLICE * e
                    grad = moe[k, row : row + SLICE].astype(f32)
                    apply(1, (2 * b + e, lanes(k, SLICE), every), grad, rates[3])
                return carry

            lax.fori_loop(0, 8, tiles, 0)
        else:
            part = step - 6
            row = 0 if n == 3 else 64 * (1 + part)

            def tiles(t, carry, n=n, part=part, row=row):
                cols = lanes(t if n == 3 else 8 * part + t)
                for h in range(2):
                    grad = late[t, 192 * h + row : 192 * h + row + 64].astype(f32)
                    apply(n, (pl.ds(64 * h, 64), cols), grad, rates[1 if n == 3 else 0])
                return carry

            lax.fori_loop(0, 8, tiles, 0)
        if step == 1:
            for load, src, dst in zip(through, passing, refs[23:25]):
                load.wait()
                stores.append(copy(src, dst))
        for i, j in ((1, 0), (2, 1), (0, 2)):
            stores.append(copy(bufs[3 * n + i].at[at], outs[3 * n + j].at[at]))
    for store in stores:
        store.wait()


def update(*arrays):
    V = pltpu.VMEM
    dims = [(EXPERTS, 128, D), (EXPERTS, FF, 128), (128, 2 * D), (128, D)]
    return pl.pallas_call(
        update_kernel,
        out_shape=(shape((2, 128, D), b16), shape((2, 128, D), f32))
        + tuple(shape(d, f32) for d in dims + [(EXPERTS, 128), (2, 128)] for _ in range(3)),
        in_specs=[ANY] * 4 + [VMEM] + [ANY] * 12 + [VMEM] * 6,
        out_specs=(ANY,) * 14 + (VMEM,) * 6,
        scratch_shapes=[V((8, 1152, 128), b16), V((8, 384, 128), b16)]
        + [V(d, f32) for d in dims for _ in range(3)]
        + [V((2, 128, D), b16), V((2, 128, D), f32), pltpu.SemaphoreType.DMA((64,))],
        compiler_params=params(),
        name="update",
    )(*arrays)


def on_device(
    tokens, segments, routes, cotangent, w_qkv, w_out, w_gateup, w_down, w_router, w_gains,
    qkv_first, qkv_second, out_first, out_second, gateup_first, gateup_second, down_first, down_second,
    router_first, router_second, gains_first, gains_second,
):
    route_lanes = jnp.pad(routes, ((0, 0), (0, 0), (0, 126)))
    cos, sin = (jnp.asarray(table) for table in rotary())
    X, R, g, WQ, WKV, WO, TL, act_one, q, KV, probs, heads, hidden, act, total, grads, PO, y_tmp, y_got = front(
        tokens, cotangent, route_lanes, w_qkv, w_out, w_gateup, w_down, cos, sin, w_router.T, w_gains, segments
    )
    layer_out, input_grad, ALLM, late, SM = back(
        total, hidden, act, g, TL, R, heads, WO, X, act_one, q, KV, probs, WQ, WKV,
        grads, PO, y_tmp, y_got, cos, sin,
    )
    done = update(
        ALLM, late, layer_out, input_grad, SM, w_gateup, gateup_first, gateup_second, w_down, down_first, down_second,
        w_qkv, qkv_first, qkv_second, w_out, out_first, out_second,
        w_router.T, router_first.T, router_second.T, w_gains, gains_first, gains_second,
    )
    router = [array.T for array in done[14:17]]
    return (*done[:2], *done[8:11], *done[11:14], *done[2:5], *done[5:8], *router, *done[17:20])


def solution(mesh):
    weight = [P("grp", None), P("grp", None), P(None, "grp", None), P(None, None, "grp"), P("grp", None), P(None, "grp")]
    tokens = P("rep", "grp", None)
    moments = [spec for spec in weight for _ in range(2)]
    results = [spec for spec in weight for _ in range(3)]
    return jax.shard_map(
        on_device,
        mesh=mesh,
        in_specs=(tokens, P("rep", None), tokens, tokens, *weight, *moments),
        out_specs=(tokens, tokens, *results),
        check_vma=False,
    )
```

profile of v0, /device:TPU:1, one launch (start us, length us, event | category | flops | bytes accessed | tf_op | source)
XLA Modules:
  0.0 209.4 jit_solution(12439028784554743963)
XLA Ops:
  0.7 0.8 copy.44
  1.5 0.7 pad.4.rl
  2.1 115.6 %front.1 = (bf16[256,1024]{1,0:T(8,128)(2,1)}, s32[256,128]{1,0:T(8,128)}, bf16[256,1024]{1,0:T(8,128)(2,1)}, bf16[1024,1024]{1,0:T(8,128)(2,1)}, bf16[1024,1024...) custom-call(bf16[2,128,1024]{2,1,0:T(8,128)(2,1)} %tok.1, ...), custom_call_target="tpu_custom_call" | custom-call | tf_op jit(solution)/shard_map/front/pallas_call | solution.py:671
  117.7 74.8 %back.1 = (bf16[2,128,1024]{2,1,0:T(8,128)(2,1)}, f32[2,128,1024]{2,1,0:T(8,128)}, bf16[8,1152,128]{2,1,0:T(8,128)(2,1)}, bf16[8,384,128]{2,1,0:T(8,128)(2,1)}, f32[8,128]{1,0:T(8,128)}) custom-call(f32[256,1152]{1,0:T(8,128)} %get-tuple-element.64.total_i, f32[256,1024]{1,0:T(8,128)} %get-tuple-element.65.hidden_i, ...), custom_call_target="tpu_custom_call" | custom-call | tf_op jit(solution)/shard_map/back/pallas_call | solution.py:1056
  192.5 16.7 %update.1 = (bf16[2,128,1024]{2,1,0:T(8,128)(2,1)}, f32[2,128,1024]{2,1,0:T(8,128)}, f32[6,128,1024]{2,1,0:T(8,128)}, f32[6,128,1024]{2,1,0:T(8,128)}, f32[6,128...) custom-call(bf16[8,1152,128]{2,1,0:T(8,128)(2,1)} %get-tuple-element, ...), custom_call_target="tpu_custom_call" | custom-call | tf_op jit(solution)/shard_map/update/pallas_call | solution.py:1248
where the time goes:
time: 210 us; the launch traced here: 209 us
  Pallas kernels  207 us (99%)
    pallas_call x1, Pallas kernels, front(): pl.pallas_call(front_kernel, out_shape=(shape((ROWS, D), b16), shape((ROW...  116 us
    pallas_call x1, Pallas kernels, back(): pl.pallas_call(back_kernel, out_shape=(shape((2, 128, D), b16), shape((2,...  74.8 us
    pallas_call x1, Pallas kernels, update(): pl.pallas_call(update_kernel, out_shape=(shape((2, 128, D), b16), shape((...  16.7 us

commit v1 on v0

--- a/solution.py
+++ b/solution.py
@@ -280,10 +280,10 @@
 
 
 def front_kernel(
-    tok, cot, rl, wqkv, wout, wgu, wdn, cos_t, sin_t, router, gains, segs,
+    tok, cot, routes_in, wqkv, wout, wgu, wdn, cos_t, sin_t, router, gains, segs,
     X_o, R_o, g_o, WQ_o, WKV_o, WO_o, TL_o, one_o, q_o, KV_o, P_o, heads_o, hidden_o, act_o, total, grads_o, PO, y_tmp, y_got,
     X, R, WQ, WKV, WO, TL, one, q, KV, probs_all, heads, hidden, ACT, G, GD, back, tw, tmp, got, gu_acc, dn_acc, grads, bias,
-    wq32, wkv32, wo32, gate32, up32, dn32, wq16, wkv16, wo16, gd16, cos, sin, tail32, tail,
+    wq32, wkv32, wo32, gate32, up32, dn32, wq16, wkv16, wo16, gd16, cos, sin, tail32, tail, rl,
     ss, rs, ls,
 ):
     x, y, z, c = place()
@@ -292,6 +292,8 @@
     net = Net(ss, rs, ls)
     kept = []
     keep = lambda src, dst: kept.append(net.local(src, dst))
+    rl[...] = jnp.zeros_like(rl)
+    rl[:, :, 0:TOPK] = routes_in[...]
     loads = [
         net.local(wqkv.at[:, pl.ds(pl.multiple_of(D + c * 512, 512), 512)], wkv32),
         net.local(wqkv.at[:, lanes(slot)], wq32),
@@ -691,7 +693,7 @@
             shape((2, 2, 576, 128), b16),
             shape((2, 2, 1152, 128), b16),
         ),
-        in_specs=[ANY] * 9 + [VMEM] * 3,
+        in_specs=[ANY] * 2 + [VMEM] + [ANY] * 6 + [VMEM] * 3,
         out_specs=(ANY,) * 14 + (VMEM,) + (ANY,) * 4,
         scratch_shapes=[
             V((ROWS, D), b16),
@@ -731,6 +733,7 @@
             V((ROWS, 128), f32),
             V((16, 128), f32),
             V((16, 128), b16),
+            V((2, 128, 128), jnp.int32),
         ]
         + sems(160, 64),
         compiler_params=params(0, 62),
@@ -1264,10 +1267,9 @@
     qkv_first, qkv_second, out_first, out_second, gateup_first, gateup_second, down_first, down_second,
     router_first, router_second, gains_first, gains_second,
 ):
-    route_lanes = jnp.pad(routes, ((0, 0), (0, 0), (0, 126)))
     cos, sin = (jnp.asarray(table) for table in rotary())
     X, R, g, WQ, WKV, WO, TL, act_one, q, KV, probs, heads, hidden, act, total, grads, PO, y_tmp, y_got = front(
-        tokens, cotangent, route_lanes, w_qkv, w_out, w_gateup, w_down, cos, sin, w_router.T, w_gains, segments
+        tokens, cotangent, routes, w_qkv, w_out, w_gateup, w_down, cos, sin, w_router.T, w_gains, segments
     )
     layer_out, input_grad, ALLM, late, SM = back(
         total, hidden, act, g, TL, R, heads, WO, X, act_one, q, KV, probs, WQ, WKV,

time: 210 us -> 210 us (level)
  no operation moved by 1% of the time
where the time goes in v1:
time: 210 us
  Pallas kernels  207 us (99%)
    pallas_call x1, Pallas kernels, front(): pl.pallas_call(front_kernel, out_shape=(shape((ROWS, D), b16), shape((ROW...  116 us
    pallas_call x1, Pallas kernels, back(): pl.pallas_call(back_kernel, out_shape=(shape((2, 128, D), b16), shape((2,...  74.8 us
    pallas_call x1, Pallas kernels, update(): pl.pallas_call(update_kernel, out_shape=(shape((2, 128, D), b16), shape((...  16.7 us

profile of v1, /device:TPU:1, one launch (start us, length us, event | category | flops | bytes accessed | tf_op | source)
XLA Modules:
  0.0 209.7 jit_solution(4152660238297149255)
XLA Ops:
  0.7 1.5 copy.44.routes_in
  2.1 115.9 %front.1 = (bf16[256,1024]{1,0:T(8,128)(2,1)}, s32[256,128]{1,0:T(8,128)}, bf16[256,1024]{1,0:T(8,128)(2,1)}, bf16[1024,1024]{1,0:T(8,128)(2,1)}, bf16[1024,1024...) custom-call(bf16[2,128,1024]{2,1,0:T(8,128)(2,1)} %tok.1, ...), custom_call_target="tpu_custom_call" | custom-call | tf_op jit(solution)/shard_map/front/pallas_call | solution.py:673
  118.0 74.8 %back.1 = (bf16[2,128,1024]{2,1,0:T(8,128)(2,1)}, f32[2,128,1024]{2,1,0:T(8,128)}, bf16[8,1152,128]{2,1,0:T(8,128)(2,1)}, bf16[8,384,128]{2,1,0:T(8,128)(2,1)}, f32[8,128]{1,0:T(8,128)}) custom-call(f32[256,1152]{1,0:T(8,128)} %get-tuple-element.64.total_i, f32[256,1024]{1,0:T(8,128)} %get-tuple-element.65.hidden_i, ...), custom_call_target="tpu_custom_call" | custom-call | tf_op jit(solution)/shard_map/back/pallas_call | solution.py:1059
  192.8 16.7 %update.1 = (bf16[2,128,1024]{2,1,0:T(8,128)(2,1)}, f32[2,128,1024]{2,1,0:T(8,128)}, f32[6,128,1024]{2,1,0:T(8,128)}, f32[6,128,1024]{2,1,0:T(8,128)}, f32[6,128...) custom-call(bf16[8,1152,128]{2,1,0:T(8,128)(2,1)} %get-tuple-element, ...), custom_call_target="tpu_custom_call" | custom-call | tf_op jit(solution)/shard_map/update/pallas_call | solution.py:1251
